TPU v7x, 32 devices: a whole 2x2x4 slice. The times are simulated.
32 devices in a mesh: replica: 2 (over x), fsdp: 16 (over z, y, core).
Axes of the slice: x: 2, y: 2, z: 4, core: 2. Of those that a mesh axis runs over, the one named last changes fastest.
Arguments:
- tokens: bfloat16 [8192, 7168], P(('replica', 'fsdp')), may hold values from -6 to 6
- cotangent: bfloat16 [8192, 128], P(('replica', 'fsdp')), may hold values from -0.09375 to 0.09375
- keep_mask: int32 [8192], P(('replica', 'fsdp')), may hold values 0 or 1
- key_weight: bfloat16 [2, 7168, 128], P('replica', 'fsdp'), may hold values from -0.0625 to 0.0625
- norm_gain: float32 [2, 7168], P('replica', 'fsdp'), may hold values from 0.1 to 1.9
- local_params: float32 [2, 8, 65536], P('replica', None, 'fsdp'), may hold values from -1400 to 1400
- global_params: float32 [8, 65536], P(None, 'fsdp'), may hold values from -4 to 4
- momentum: float32 [8, 65536], P(None, 'fsdp'), may hold values from -6 to 6
- fragment_order: int32 [8], replicated, may hold values from 0 to 7, each once
Outputs:
- weight_grad: float32 [2, 7168, 128], P('replica', 'fsdp')
- gain_grad: float32 [2, 7168], P('replica', 'fsdp')
- local_out: float32 [2, 8, 65536], P('replica', None, 'fsdp')
- global_out: float32 [8, 65536], P(None, 'fsdp')
- moment_out: float32 [8, 65536], P(None, 'fsdp')
Inputs may be any that keep to these rules, and one draw needn't show every extreme that they name: `fragment_order`: its first 2 entries name the fragment's layers.
All inputs are finite; a program needn't handle non-finite values. No bound on the sum of `keep_mask` on one device may be relied on, other than what follows from the above.
Results may differ from a plain program's by a relative error of at most 0.005.
Values may be sent and summed in bfloat16 or wider, within the bound.
No kernel may reach another device: no remote copies, remote signals or barrier semaphores. Data moves between devices by JAX's collectives and lax.ppermute only.
A program may use at most 64 MiB of HBM per device.

v0:
```python
import jax
import jax.numpy as jnp
from jax import lax
from jax.sharding import PartitionSpec as P

FRAG = 2


EPSILON = 1e-06
CLIP_RATE = 0.5
MOMENT = 0.9
OUTER_RATE = 0.7
MIX_RATE = 0.5


def outer_step(averaged, glob_rows, moment_rows, squares, count):
    limit = CLIP_RATE * jnp.sqrt(jnp.float32(count))
    factor = jnp.minimum(1.0, limit / jnp.sqrt(squares + EPSILON))
    clipped = averaged * factor
    moment_new = MOMENT * moment_rows + clipped
    global_new = glob_rows - OUTER_RATE * (clipped + MOMENT * moment_new)
    return (moment_new, global_new)


def inner_part(tokens, cotangent, keep_mask, key_weight, norm_gain):
    as_float = tokens.astype(jnp.float32)
    inv_rms = lax.rsqrt(jnp.mean(as_float * as_float, axis=1, keepdims=True) + EPSILON)
    unit_rows = as_float * inv_rms
    normed = unit_rows.astype(jnp.bfloat16)
    masked = jnp.where(keep_mask[:, None] == 1, cotangent, jnp.zeros_like(cotangent))
    hidden_grad = jnp.einsum(
        "th,dh->td",
        masked,
        lax.all_gather(key_weight[0], "fsdp", axis=0, tiled=True),
        preferred_element_type=jnp.float32,
    )
    gain_partial = jnp.sum(hidden_grad * unit_rows, axis=0)
    partial_grad = jnp.einsum("td,th->dh", normed, masked, preferred_element_type=jnp.float32)
    own_grad, gain_grad = (
        lax.psum_scatter(partial_grad, "fsdp", scatter_dimension=0, tiled=True),
        lax.psum_scatter(gain_partial, "fsdp", scatter_dimension=0, tiled=True),
    )
    weight_grad = (norm_gain[0][:, None] * own_grad)[None]
    return (weight_grad, gain_grad[None])


def outer_part(local_params, global_params, momentum, fragment_order):
    frag_rows = fragment_order[:FRAG]
    own_local = local_params[0]
    local_rows = jnp.take(own_local, frag_rows, axis=0)
    glob_rows = jnp.take(global_params, frag_rows, axis=0)
    moment_rows = jnp.take(momentum, frag_rows, axis=0)
    delta = glob_rows - local_rows
    replicas = lax.axis_size("replica")
    count = FRAG * global_params.shape[1] * lax.axis_size("fsdp")
    averaged = lax.psum(delta.astype(jnp.bfloat16), "replica").astype(jnp.float32) / replicas
    squares = lax.psum(jnp.sum(averaged * averaged), "fsdp")
    moment_new, global_new = outer_step(averaged, glob_rows, moment_rows, squares, count)
    merged = MIX_RATE * local_rows + (1.0 - MIX_RATE) * global_new
    local_out = own_local.at[frag_rows].set(merged)[None]
    global_out = global_params.at[frag_rows].set(global_new)
    moment_out = momentum.at[frag_rows].set(moment_new)
    return (local_out, global_out, moment_out)


def per_device(
    tokens,
    cotangent,
    keep_mask,
    key_weight,
    norm_gain,
    local_params,
    global_params,
    momentum,
    fragment_order,
):
    weight_grad, gain_grad = inner_part(tokens, cotangent, keep_mask, key_weight, norm_gain)
    local_out, global_out, moment_out = outer_part(
        local_params, global_params, momentum, fragment_order
    )
    return (weight_grad, gain_grad, local_out, global_out, moment_out)


def solution(mesh):
    in_specs = (
        P(("replica", "fsdp"), None),
        P(("replica", "fsdp"), None),
        P(("replica", "fsdp")),
        P("replica", "fsdp", None),
        P("replica", "fsdp"),
        P("replica", None, "fsdp"),
        P(None, "fsdp"),
        P(None, "fsdp"),
        P(),
    )
    out_specs = (
        P("replica", "fsdp", None),
        P("replica", "fsdp"),
        P("replica", None, "fsdp"),
        P(None, "fsdp"),
        P(None, "fsdp"),
    )
    return jax.shard_map(
        per_device, mesh=mesh, in_specs=in_specs, out_specs=out_specs, check_vma=False
    )
```

profile of v0, /device:TPU:0, one launch (start us, length us, event | category | flops | bytes accessed | tf_op | source)
XLA Modules:
  0.0 133.7 jit_solution(16027352460616817769)
XLA Ops:
  7.2 0.0 all-gather.3.cloned.1.call-start
  7.2 0.9 copy.20
  8.1 0.9 copy.21
  9.0 0.9 copy.22
  9.9 0.0 all-gather.3.cloned.1.call-update
  10.0 0.0 reduce-scatter.2.cloned.1.call-start
  10.0 0.0 copy-start
  10.0 0.8 broadcast_compare_fusion
  10.9 3.0 %fusion.1 = f32[256]{0:T(256)S(1)} fusion(bf16[256,7168]{1,0:T(8,128)(2,1)} %param.11), kind=kLoop, calls=%fused_computation.10 | loop fusion | flops 5504768 | bytes 3671040 | tf_op jit(solution)/shard_map/reduce_sum | solution.py:27
  13.9 3.3 %fusion.2 = f32[7168,128]{1,0:T(8,128)} fusion(bf16[256,7168]{1,0:T(8,128)(2,1)S(1)} %copy-done, f32[256]{0:T(256)S(1)} %add_rsqrt_fusion, bf16[256,128]{1,0:T(8,128)(2,1)S(1)} %copy-done.4, pred[256]{0:T(512)(128)(4,1)S(1)} %broadcast_compare_fusion), kind=kOutput, calls=%fused_computation.11 | convolution fusion | flops 475299840 | bytes 7406848 | tf_op jit(solution)/shard_map/td,th->dh/dot_general | solution.py:38
  17.2 0.0 reduce-scatter.2.cloned.1.call-update
  17.2 0.6 copy-done.6
  17.9 0.6 gather_fusion
  18.4 0.6 gather_fusion.1
  19.0 0.6 gather_fusion.2
  19.6 0.0 copy-done.7
  19.6 0.6 dynamic-slice
  20.9 0.1 subtract_convert_fusion
  21.0 9.7 %psum.14 = bf16[2,4096]{1,0:T(2,128)(2,1)S(1)} all-reduce(bf16[2,4096]{1,0:T(2,128)(2,1)S(1)} %subtract_convert_fusion), channel_id=1, replica_groups=mesh['replica'=2,'fsdp'=16] {'replica'}, use_global_device_ids=true, to_apply=%region_4.6 | all-reduce | flops 8192 | bytes 32768 | tf_op jit(solution)/shard_map/psum | solution.py:56
  30.6 0.6 fusion.12
  31.2 22.3 %all-gather.3.cloned.1.call-done = bf16[1,7168,128]{2,1,0:T(8,128)(2,1)} async-done(((bf16[1,448,128]{2,1,0:T(8,128)(2,1)}), bf16[1,7168,128]{2,1,0:T(8,128)(2,1)}) %all-gather.3.cloned.1.call-update) | async-done | bytes 1835024 | tf_op jit(solution)/shard_map/all_gather | solution.py:34
  53.6 3.8 %fusion.5 = f32[7168]{0:T(1024)S(1)} fusion(f32[256]{0:T(256)S(1)} %add_rsqrt_fusion, bf16[256,7168]{1,0:T(8,128)(2,1)} %param.11, bf16[1,7168,128]{2,1,0:T(8,128)(2,1)} %all-gather.3.cloned.1.call-done, bf16[256,128]{1,0:T(8,128)(2,1)S(1)} %copy-done.4, pred[256]{0:T(512)(128)(4,1)S(1)} %broadcast_compare_fusion), kind=kOutput, calls=%fused_computation.13 | convolution fusion | flops 477127680 | bytes 5600512 | tf_op jit(solution)/shard_map/th,dh->td/dot_general | solution.py:31
  57.4 60.2 %all-reduce.1 = (f32[7168]{0:T(1024)S(1)}, f32[]{:T(128)}) all-reduce(f32[7168]{0:T(1024)S(1)} %fusion.5, f32[]{:T(128)} %fusion.12), channel_id=4, replica_groups=mesh['replica'=2,'fsdp'=16] {'fsdp'}, use_global_device_ids=true, to_apply=%region_3.4.clone | all-reduce | flops 7169 | bytes 57352
  118.2 0.8 scatter_custom_fusion
  119.1 0.0 copy-start.3
  119.1 0.8 scatter_custom_fusion.1
  119.9 0.0 copy-start.2
  119.9 0.8 scatter_custom_fusion.2
  120.7 0.0 copy-start.1
  120.7 0.7 dynamic-slice.1
  121.4 3.7 %reduce-scatter.2.cloned.1.call-done = f32[448,128]{1,0:T(8,128)} async-done(((f32[7168,128]{1,0:T(8,128)}), f32[448,128]{1,0:T(8,128)}) %reduce-scatter.2.cloned.1.call-update) | async-done | bytes 229392 | tf_op jit(solution)/shard_map/reduce_scatter | solution.py:40
  125.1 1.8 %multiply_bitcast_fusion = f32[1,448,128]{2,1,0:T(8,128)} fusion(f32[448,128]{1,0:T(8,128)} %reduce-scatter.2.cloned.1.call-done, f32[448]{0:T(512)S(1)} %bitcast.13), kind=kLoop, calls=%fused_computation.15 | loop fusion | flops 57344 | bytes 460544 | tf_op jit(solution)/shard_map/broadcast_in_dim | solution.py:43
  (13 shorter events, 0.0 us)
Async XLA Ops:
  7.2 6.7 %copy-start.4 = (bf16[256,128]{1,0:T(8,128)(2,1)S(1)}, bf16[256,128]{1,0:T(8,128)(2,1)}, u32[]{:S(2)}) copy-start(bf16[256,128]{1,0:T(8,128)(2,1)} %param.12) | copy-start | bytes 196612
  7.2 46.4 %all-gather.3.cloned.1.call-start = ((), (), s32[]{:S(2)}) async-start(), calls=%async_computation.2 | async-start | bytes 1949696 | tf_op jit(solution)/shard_map/all_gather | solution.py:34
  10.0 115.2 %reduce-scatter.2.cloned.1.call-start = ((), (), s32[]{:S(2)}) async-start(), calls=%async_computation.1 | async-start | bytes 3899392 | tf_op jit(solution)/shard_map/reduce_scatter | solution.py:40
  10.0 3.9 %copy-start = (bf16[256,7168]{1,0:T(8,128)(2,1)S(1)}, bf16[256,7168]{1,0:T(8,128)(2,1)}, u32[]{:S(2)}) copy-start(bf16[256,7168]{1,0:T(8,128)(2,1)} %param.11) | copy-start | bytes 11010052
  17.2 0.7 copy-start.6
  17.2 2.4 %copy-start.7 = (u32[32]{0:T(128)S(1)}, u32[32]{0:T(128)}, u32[]{:S(2)}) copy-start(u32[32]{0:T(128)} %constant.43) | copy-start | bytes 388
  31.2 93.9 %copy-start.5 = (f32[1,448]{1,0:T(1,128)S(1)}, f32[1,448]{1,0:T(1,128)}, u32[]{:S(2)}) copy-start(f32[1,448]{1,0:T(1,128)} %param.15) | copy-start | bytes 5380
  119.1 7.8 %copy-start.3 = (f32[8,4096]{1,0:T(8,128)}, f32[8,4096]{1,0:T(8,128)S(1)}, u32[]{:S(2)}) copy-start(f32[8,4096]{1,0:T(8,128)S(1)} %scatter_custom_fusion) | copy-start | bytes 393220
  119.9 7.0 %copy-start.2 = (f32[8,4096]{1,0:T(8,128)}, f32[8,4096]{1,0:T(8,128)S(1)}, u32[]{:S(2)}) copy-start(f32[8,4096]{1,0:T(8,128)S(1)} %scatter_custom_fusion.1) | copy-start | bytes 393220
  120.7 6.2 %copy-start.1 = (f32[8,4096]{1,0:T(8,128)}, f32[8,4096]{1,0:T(8,128)S(1)}, u32[]{:S(2)}) copy-start(f32[8,4096]{1,0:T(8,128)S(1)} %scatter_custom_fusion.2) | copy-start | bytes 393220
Sparse Core Ops, SparseCore 0:
  10.3 43.2 all-gather.2
  57.4 67.6 reduce-scatter.1
where the time goes:
time: 134 us
  blocking collectives  69.8 us (52%)
  waiting for transfers between devices  26.1 us (19%)
  between operations  15.5 us (12%)
  other arithmetic  8.8 us (7%)
  matrix products  7.06 us (5%)
  local copies, waits for them, and re-layouts  6.34 us (5%)
    unnamed x1, blocking collectives  60.2 us
    all_gather x1, waiting for transfers between devices, inner_part(): lax.all_gather(key_weight[0], 'fsdp', axis=0, tiled=True)  22.3 us
    psum x1, blocking collectives, outer_part(): lax.psum(delta.astype(jnp.bfloat16), 'replica').astype(jnp.float32)  9.66 us
    unnamed x21, local copies, waits for them, and re-layouts  4.62 us
    dot_general x1, matrix products, inner_part(): jnp.einsum('th,dh->td', masked, lax.all_gather(key_weight[0], 'fsdp', axi...  3.78 us
    reduce_scatter x1, waiting for transfers between devices, inner_part(): lax.psum_scatter(partial_grad, 'fsdp', scatter_dimension=0, tiled=True)  3.74 us
    dot_general x1, matrix products, inner_part(): jnp.einsum('td,th->dh', normed, masked, preferred_element_type=jnp.float32)  3.28 us
    reduce_sum x1, other arithmetic, inner_part(): jnp.mean(as_float * as_float, axis=1, keepdims=True) + EPSILON  3.03 us
  transfers between devices with their start and end apart: 2, of which 2 were waited for; matrix products, arithmetic and copies ran while one was open for 13% of the time, Pallas kernels for 0%

commit v1 on v0

--- a/solution.py
+++ b/solution.py
@@ -1,6 +1,10 @@
+import functools
+
 import jax
 import jax.numpy as jnp
 from jax import lax
+from jax.experimental import pallas as pl
+from jax.experimental.pallas import tpu as pltpu
 from jax.sharding import PartitionSpec as P
 
 FRAG = 2
@@ -11,6 +15,397 @@
 MOMENT = 0.9
 OUTER_RATE = 0.7
 MIX_RATE = 0.5
+
+LANES = 128
+PACKED_ROWS = 16
+ROW_BLOCK = 32
+MIB = 1024 * 1024
+
+
+def fsdp_factors(count):
+    factors = []
+    for factor in (2, 2):
+        if count % factor == 0:
+            factors.append(factor)
+            count //= factor
+    while count % 4 == 0:
+        factors.append(4)
+        count //= 4
+    while count % 2 == 0:
+        factors.append(2)
+        count //= 2
+    assert count == 1
+    return factors
+
+
+def xor_pairs(count, mask):
+    return [(i, i ^ mask) for i in range(count)]
+
+
+def swap(array, mask):
+    return lax.ppermute(array, "fsdp", xor_pairs(lax.axis_size("fsdp"), mask))
+
+
+def cross_swap(array, even, odd):
+    count = lax.axis_size("fsdp")
+    return lax.ppermute(array, "fsdp", [(i, i ^ (odd if i % 2 else even)) for i in range(count)])
+
+
+VMEM = pl.BlockSpec(memory_space=pltpu.VMEM)
+SMEM = pl.BlockSpec(memory_space=pltpu.SMEM)
+HBM = pl.BlockSpec(memory_space=pltpu.HBM)
+ANY = pl.BlockSpec(memory_space=pl.ANY)
+
+
+def local_call(kernel, name, outs, in_specs, vmem_mib, scratch=(), out_spec=VMEM, moved=0, aliases=None):
+    return pl.pallas_call(
+        kernel,
+        name=name,
+        out_shape=[jax.ShapeDtypeStruct(shape, dtype) for shape, dtype in outs],
+        in_specs=in_specs,
+        out_specs=[out_spec] * len(outs),
+        scratch_shapes=list(scratch),
+        input_output_aliases=aliases or {},
+        cost_estimate=pl.CostEstimate(flops=0, bytes_accessed=moved, transcendentals=0),
+        compiler_params=pltpu.CompilerParams(vmem_limit_bytes=vmem_mib * MIB),
+    )
+
+
+def in_hbm(array):
+    return pltpu.with_memory_space_constraint(array, pltpu.HBM)
+
+
+def squares_tile(squares):
+    value = squares[0:1, :]
+    pieces = []
+    for _ in range(3):
+        piece = value.astype(jnp.bfloat16).astype(jnp.float32)
+        pieces.append(piece)
+        value = value - piece
+    pieces.append(jnp.zeros((PACKED_ROWS - 3, LANES), jnp.float32))
+    return jnp.concatenate(pieces, axis=0).astype(jnp.bfloat16)
+
+
+def tile_squares(tile):
+    tile = tile.astype(jnp.float32)
+    return (tile[0:1] + tile[1:2]) + tile[2:3]
+
+
+def rows_kernel(tokens, cotangent, mask, order, local_params, global_params, held, left, delta, squares, cot, keep, at, own, shared, sems, more):
+    rows, width = held.shape
+    blocks = rows // ROW_BLOCK
+    copies = []
+    small = [
+        pltpu.make_async_copy(source, target, more.at[i])
+        for i, (source, target) in enumerate(
+            ((order, at), (global_params, shared), (local_params, own), (cotangent, cot), (mask, keep))
+        )
+    ]
+    small[0].start()
+    for i in range(blocks):
+        here = pl.ds(i * ROW_BLOCK, ROW_BLOCK)
+        copies.append(pltpu.make_async_copy(tokens.at[here], held.at[here], sems.at[i]))
+        copies[-1].start()
+        if i == 0:
+            for copy in small[1:]:
+                copy.start()
+    for i, copy in enumerate(copies):
+        if i == blocks // 2:
+            for other in small:
+                other.wait()
+            picked = []
+            for j in range(FRAG):
+                row = pl.ds(at[j], 1)
+                picked.append(shared[row, :] - own[0, row, :])
+            delta[...] = jnp.concatenate(picked, axis=0).astype(jnp.bfloat16)
+            cot_t = cot[...].astype(jnp.float32).T
+        copy.wait()
+        here = pl.ds(i * ROW_BLOCK, ROW_BLOCK)
+        totals = [jnp.zeros((ROW_BLOCK, LANES), jnp.float32)] * 4
+        for j in range(width // LANES):
+            part = held[here, j * LANES : (j + 1) * LANES].astype(jnp.float32)
+            totals[j % 4] = totals[j % 4] + part * part
+        squares[here, :] = (totals[0] + totals[1]) + (totals[2] + totals[3])
+    mean = jnp.sum(squares[...].T, axis=0, keepdims=True) * (1.0 / width)
+    scale = jnp.where(keep[...] == 1, lax.rsqrt(mean + EPSILON), 0.0)
+    scaled = cot_t * scale
+    high = scaled.astype(jnp.bfloat16)
+    low = (scaled - high.astype(jnp.float32)).astype(jnp.bfloat16)
+    left[...] = jnp.concatenate([high, low], axis=0)
+
+
+def place_bits():
+    index = lax.axis_index("fsdp")
+    core = lax.rem(index, 2)
+    y = lax.rem(index // 2, 2)
+    near = lax.rem(index // 4, 2)
+    straight = core == 0
+    return straight, jnp.where(straight, y, near), jnp.where(straight, near, y)
+
+
+def partial_kernel(tiles, own_half, held, left, send, keep):
+    heads = send.shape[2]
+    chunk = tiles * PACKED_ROWS
+    index = lax.axis_index("fsdp")
+    first = lax.rem(index, 2) == 0
+    half = index // 8 if own_half else 1 - index // 8
+    for k in range(4):
+        start = pl.multiple_of(half * (8 * chunk) + k * 2 * chunk, LANES)
+        both = jnp.dot(
+            left[...], held[:, pl.ds(start, 2 * chunk)], preferred_element_type=jnp.float32
+        )
+        sums = (both[:heads] + both[heads:]).T.reshape(2, tiles, PACKED_ROWS, heads)
+        here = slice(k * tiles, (k + 1) * tiles)
+        send[here] = jnp.where(first, sums[1], sums[0]).astype(jnp.bfloat16)
+        keep[here] = jnp.where(first, sums[0], sums[1])
+
+
+def spread_kernel(gain, after, spread):
+    spread[...] = jnp.broadcast_to(gain[...], spread.shape[::-1]).T
+
+
+def squares_kernel(own, other, after, squares):
+    mean = (own[...].astype(jnp.float32) + other[...].astype(jnp.float32)) * 0.5
+    squares[...] = jnp.broadcast_to(jnp.sum(mean * mean), squares.shape)
+
+
+def pass_squares(squares, came, send, squares_sum):
+    both = squares[...] + tile_squares(came[came.shape[0] - 1])
+    squares_sum[...] = both
+    if send is not None:
+        send[send.shape[0] - 1] = squares_tile(both)
+
+
+def first_kernel(keep, came, *rest):
+    tiles = keep.shape[0] // 4
+    straight, own, _ = place_bits()
+    if len(rest) == 5:
+        squares, squares_came, send, kept, squares_sum = rest
+        both = squares[...] + squares_came[...]
+        squares_sum[...] = both
+        send[2 * tiles] = squares_tile(both)
+    else:
+        send, kept = rest
+
+    def total(bit, other):
+        place = jnp.where(straight, bit + 2 * other, 2 * bit + other)
+        there = pl.ds(place * tiles, tiles)
+        return keep[there] + came[there].astype(jnp.float32)
+
+    for other in range(2):
+        here = slice(other * tiles, (other + 1) * tiles)
+        send[here] = total(1 - own, other).astype(jnp.bfloat16)
+        kept[here] = total(own, other)
+
+
+def first_far_kernel(keep, came, after, passing, send, kept, passed):
+    first_kernel(keep, came, send, kept)
+
+
+def second_kernel(keep, came, *rest):
+    squares, send, kept, squares_sum = rest if len(rest) == 4 else (None, *rest, None)
+    tiles = keep.shape[0] // 2
+    _, _, own = place_bits()
+    if squares is not None:
+        pass_squares(squares, came, send, squares_sum)
+
+    def total(bit):
+        there = pl.ds(bit * tiles, tiles)
+        return keep[there] + came[there].astype(jnp.float32)
+
+    send[:tiles] = total(1 - own).astype(jnp.bfloat16)
+    kept[...] = total(own)
+
+
+def third_kernel(keep, came, squares, send):
+    tiles = keep.shape[0]
+    send[:tiles] = (keep[...] + came[...].astype(jnp.float32)).astype(jnp.bfloat16)
+    send[tiles] = squares_tile(squares[...])
+
+
+def prepare_kernel(keep, came, squares, order, own, other, local_params, global_params, momentum, kept, squares_sum, local_base, global_base, moment_base, local_slope, global_slope, moment_slope):
+    pass_squares(squares, came, None, squares_sum)
+    kept[...] = keep[...] + came[: keep.shape[0]].astype(jnp.float32)
+    local_base[...] = local_params[...]
+    global_base[...] = global_params[...]
+    moment_base[...] = momentum[...]
+    for slope in (local_slope, global_slope, moment_slope):
+        slope[...] = jnp.zeros_like(slope)
+    mean = (own[...].astype(jnp.float32) + other[...].astype(jnp.float32)) * 0.5
+    for i in range(FRAG):
+        row = pl.ds(order[i], 1)
+        averaged = mean[i : i + 1, :]
+        moment_kept = MOMENT * momentum[row, :]
+        global_kept = global_params[row, :] - OUTER_RATE * MOMENT * moment_kept
+        global_step = -(OUTER_RATE * (1.0 + MOMENT)) * averaged
+        moment_base[row, :] = moment_kept
+        moment_slope[row, :] = averaged
+        global_base[row, :] = global_kept
+        global_slope[row, :] = global_step
+        local_base[0, row, :] = MIX_RATE * local_params[0, row, :] + (1.0 - MIX_RATE) * global_kept
+        local_slope[0, row, :] = (1.0 - MIX_RATE) * global_step
+
+
+def last_kernel(count, keep, came, squares, squares_came, weight, spread, local_base, global_base, moment_base, local_slope, global_slope, moment_slope, weight_grad, gain_grad, local_out, global_out, moment_out, grad_held, gain_held, local_held, global_held, moment_held, sems):
+    tiles = keep.shape[0]
+    copies = []
+
+    def put(source, target):
+        copies.append(pltpu.make_async_copy(source, target, sems.at[len(copies)]))
+        copies[-1].start()
+
+    grad = (keep[...] + came[:tiles].astype(jnp.float32)).reshape(weight.shape[1:])
+    grad_held[0] = grad * spread[...]
+    put(grad_held, weight_grad)
+    total = squares[0:1, :] + (tile_squares(came[tiles]) + squares_came[0:1, :])
+    limit = CLIP_RATE * count**0.5
+    factor = jnp.minimum(1.0, limit / jnp.sqrt(total[:, 0:1] + EPSILON))
+    local_held[0] = local_base[0] + factor * local_slope[0]
+    put(local_held, local_out)
+    global_held[...] = global_base[...] + factor * global_slope[...]
+    put(global_held, global_out)
+    moment_held[...] = moment_base[...] + factor * moment_slope[...]
+    put(moment_held, moment_out)
+    products = (grad * weight[0].astype(jnp.float32)).T
+    gain_held[...] = jnp.sum(products, axis=0, keepdims=True)
+    put(gain_held, gain_grad)
+    for copy in copies:
+        copy.wait()
+
+
+def three_stage(tokens, cotangent, keep_mask, key_weight, norm_gain, local_params, global_params, momentum, fragment_order):
+    rows, features = tokens.shape
+    chunk, heads = key_weight.shape[1:]
+    tiles = chunk // PACKED_ROWS
+    width = global_params.shape[1]
+    bf16, f32 = jnp.bfloat16, jnp.float32
+    row_sum = ((8, LANES), f32)
+
+    def blocks(count, dtype):
+        return ((count, PACKED_ROWS, heads), dtype)
+
+    held, left, delta = local_call(
+        rows_kernel,
+        "token_rows",
+        [((rows, features), bf16), ((2 * heads, rows), bf16), ((FRAG, width), bf16)],
+        [HBM] * 6,
+        24,
+        [
+            pltpu.VMEM((rows, LANES), f32),
+            pltpu.VMEM((rows, heads), bf16),
+            pltpu.VMEM((1, rows), jnp.int32),
+            pltpu.SMEM(fragment_order.shape, jnp.int32),
+            pltpu.VMEM(local_params.shape, f32),
+            pltpu.VMEM(global_params.shape, f32),
+            pltpu.SemaphoreType.DMA((rows // ROW_BLOCK,)),
+            pltpu.SemaphoreType.DMA((5,)),
+        ],
+    )(*map(in_hbm, (tokens, cotangent, keep_mask[None], fragment_order, local_params, global_params)))
+    other = lax.ppermute(delta, "replica", [(0, 1), (1, 0)])
+
+    def partial(own_half):
+        return local_call(
+            functools.partial(partial_kernel, tiles, own_half),
+            "partial_own" if own_half else "partial_far",
+            [blocks(4 * tiles, bf16), blocks(4 * tiles, f32)],
+            [VMEM] * 2,
+            16,
+            moved=4 * MIB,
+        )(held, left)
+
+    far_send, far_keep = partial(False)
+    far_came = swap(far_send, 1)
+    own_send, own_keep = partial(True)
+
+    far_send, far_keep, own_send = local_call(
+        first_far_kernel,
+        "first_far",
+        [blocks(2 * tiles, bf16), blocks(2 * tiles, f32), blocks(4 * tiles, bf16)],
+        [VMEM] * 2 + [ANY, VMEM],
+        8,
+        aliases={3: 2},
+    )(far_keep, far_came, other, pltpu.with_memory_space_constraint(own_send, pltpu.VMEM))
+    far_came = cross_swap(far_send, 2, 4)
+    own_came = swap(own_send, 1)
+
+    (spread,) = local_call(
+        spread_kernel, "gain_spread", [((chunk, heads), f32)], [VMEM, ANY], 4, moved=8 * MIB
+    )(norm_gain, far_send)
+    (squares,) = local_call(
+        squares_kernel, "squares", [row_sum], [VMEM] * 2 + [ANY], 4
+    )(delta, other, spread)
+    squares_came = swap(squares, 1)
+    own_send, own_keep, squares = local_call(
+        first_kernel, "first_own", [blocks(2 * tiles + 1, bf16), blocks(2 * tiles, f32), row_sum], [VMEM] * 4, 8
+    )(own_keep, own_came, squares, squares_came)
+    own_came = cross_swap(own_send, 2, 4)
+
+    far_send, far_keep = local_call(
+        second_kernel, "second_far", [blocks(tiles, bf16), blocks(tiles, f32)], [VMEM] * 2, 8
+    )(far_keep, far_came)
+    far_came = cross_swap(far_send, 4, 2)
+    own_send, own_keep, squares = local_call(
+        second_kernel, "second_own", [blocks(tiles + 1, bf16), blocks(tiles, f32), row_sum], [VMEM] * 3, 8
+    )(own_keep, own_came, squares)
+    own_came = cross_swap(own_send, 4, 2)
+
+    (far_send,) = local_call(
+        third_kernel, "third_far", [blocks(tiles + 1, bf16)], [VMEM] * 3, 8
+    )(far_keep, far_came, squares)
+    far_came = swap(far_send, 8)
+    squares_came = cross_swap(squares, 12, 10)
+
+    states = [(local_params.shape, f32), (global_params.shape, f32), (momentum.shape, f32)]
+    own_keep, squares, *parts = local_call(
+        prepare_kernel,
+        "prepare_ends",
+        [blocks(tiles, f32), row_sum] + states + states,
+        [VMEM] * 3 + [SMEM] + [VMEM] * 5,
+        8,
+    )(own_keep, own_came, squares, fragment_order, delta, other, local_params, global_params, momentum)
+
+    count = FRAG * width * lax.axis_size("fsdp")
+    return local_call(
+        functools.partial(last_kernel, count),
+        "both_ends",
+        [((1, chunk, heads), f32), ((1, chunk), f32)] + states,
+        [VMEM] * 12,
+        8,
+        [pltpu.VMEM((1, chunk, heads), f32), pltpu.VMEM((1, chunk), f32)]
+        + [pltpu.VMEM(shape, dtype) for shape, dtype in states]
+        + [pltpu.SemaphoreType.DMA((5,))],
+        HBM,
+    )(own_keep, far_came, squares, squares_came, key_weight, spread, *parts)
+
+
+def scatter_sum(partial):
+    count = lax.axis_size("fsdp")
+    factors = fsdp_factors(count)
+    place = lax.axis_index("fsdp")
+    rest = partial.reshape(tuple(reversed(factors)) + (partial.shape[0] // count, partial.shape[1]))
+    stride = 1
+    for factor in factors:
+        axis = rest.ndim - 3
+        own = (place // stride) % factor
+        arrived = []
+        for offset in range(1, factor):
+            block = lax.dynamic_index_in_dim(rest, own ^ offset, axis, keepdims=False)
+            arrived.append(swap(block.astype(jnp.bfloat16), offset * stride))
+        total = lax.dynamic_index_in_dim(rest, own, axis, keepdims=False)
+        for block in arrived:
+            total = total + block.astype(jnp.float32)
+        rest = total
+        stride *= factor
+    return rest
+
+
+def scalar_sum(value):
+    count = lax.axis_size("fsdp")
+    mask = 1
+    while mask < count:
+        value = value + swap(value, mask)
+        mask *= 2
+    return value
 
 
 def outer_step(averaged, glob_rows, moment_rows, squares, count):
@@ -28,18 +423,9 @@
     unit_rows = as_float * inv_rms
     normed = unit_rows.astype(jnp.bfloat16)
     masked = jnp.where(keep_mask[:, None] == 1, cotangent, jnp.zeros_like(cotangent))
-    hidden_grad = jnp.einsum(
-        "th,dh->td",
-        masked,
-        lax.all_gather(key_weight[0], "fsdp", axis=0, tiled=True),
-        preferred_element_type=jnp.float32,
-    )
-    gain_partial = jnp.sum(hidden_grad * unit_rows, axis=0)
     partial_grad = jnp.einsum("td,th->dh", normed, masked, preferred_element_type=jnp.float32)
-    own_grad, gain_grad = (
-        lax.psum_scatter(partial_grad, "fsdp", scatter_dimension=0, tiled=True),
-        lax.psum_scatter(gain_partial, "fsdp", scatter_dimension=0, tiled=True),
-    )
+    own_grad = scatter_sum(partial_grad)
+    gain_grad = jnp.sum(own_grad * key_weight[0].astype(jnp.float32), axis=1)
     weight_grad = (norm_gain[0][:, None] * own_grad)[None]
     return (weight_grad, gain_grad[None])
 
@@ -53,8 +439,9 @@
     delta = glob_rows - local_rows
     replicas = lax.axis_size("replica")
     count = FRAG * global_params.shape[1] * lax.axis_size("fsdp")
-    averaged = lax.psum(delta.astype(jnp.bfloat16), "replica").astype(jnp.float32) / replicas
-    squares = lax.psum(jnp.sum(averaged * averaged), "fsdp")
+    gathered = lax.all_gather(delta.astype(jnp.bfloat16), "replica", axis=0)
+    averaged = jnp.sum(gathered.astype(jnp.float32), axis=0) / replicas
+    squares = scalar_sum(jnp.sum(averaged * averaged))
     moment_new, global_new = outer_step(averaged, glob_rows, moment_rows, squares, count)
     merged = MIX_RATE * local_rows + (1.0 - MIX_RATE) * global_new
     local_out = own_local.at[frag_rows].set(merged)[None]
@@ -74,6 +461,21 @@
     momentum,
     fragment_order,
 ):
+    chunk = key_weight.shape[1]
+    three_stages = fsdp_factors(lax.axis_size("fsdp")) == [2, 2, 4]
+    aligned = chunk % PACKED_ROWS == 0 and (2 * chunk) % LANES == 0
+    if three_stages and aligned and lax.axis_size("replica") == 2:
+        return three_stage(
+            tokens,
+            cotangent,
+            keep_mask,
+            key_weight,
+            norm_gain,
+            local_params,
+            global_params,
+            momentum,
+            fragment_order,
+        )
     weight_grad, gain_grad = inner_part(tokens, cotangent, keep_mask, key_weight, norm_gain)
     local_out, global_out, moment_out = outer_part(
         local_params, global_params, momentum, fragment_order

time: 134 us -> 30.6 us (0.23)
  blocking collectives: 69.8 us -> 0 us
  waiting for transfers between devices: 26.1 us -> 9.71 us
  between operations: 15.5 us -> 0.77 us
  starting transfers between devices: 0.08 us -> 13.6 us
  other arithmetic: 8.8 us -> 0 us
  matrix products: 7.06 us -> 0 us
  local copies, waits for them, and re-layouts: 6.34 us -> 0.04 us
  Pallas kernels: 0 us -> 6.26 us
    unnamed x1 -> x0, blocking collectives: 60.2 us -> none
    all_gather x1 -> x0, waiting for transfers between devices: 22.3 us -> none  [inner_part(): lax.all_gather(key_weight[0], 'fsdp', axis=0, tiled=True)]
    ppermute x0 -> x10, starting transfers between devices: none -> 13.6 us  [the longest x5 7.57 us: cross_swap(): lax.ppermute(array, 'fsdp', [(i, i ^ (odd if i % 2 else even)) for i in r...]
    ppermute x0 -> x10, waiting for transfers between devices: none -> 9.71 us  [the longest x5 7.91 us: cross_swap(): lax.ppermute(array, 'fsdp', [(i, i ^ (odd if i % 2 else even)) for i in r...]
    psum x1 -> x0, blocking collectives: 9.66 us -> none  [outer_part(): lax.psum(delta.astype(jnp.bfloat16), 'replica').astype(jnp.float32)]
    dot_general x2 -> x0, matrix products: 7.06 us -> none  [the longest x1 3.78 us: inner_part(): jnp.einsum('th,dh->td', masked, lax.all_gather(key_weight[0], 'fsdp', axi...]
    pallas_call x0 -> x12, Pallas kernels: none -> 6.26 us  [the longest x1 2.46 us: three_stage(): local_call(rows_kernel, 'token_rows', [((rows, features), bf16), ((2 * he...]
    unnamed x21 -> x12, local copies, waits for them, and re-layouts: 4.62 us -> 0.04 us
  transfers between devices with their start and end apart: 2 -> 10, of which waited for: 2 -> 6; matrix products, arithmetic and copies ran while one was open for 13% -> 0% of each run, Pallas kernels for 0% -> 7%
where the time goes in v1:
time: 30.6 us; the launch traced here: 30.4 us
  starting transfers between devices  13.6 us (44%)
  waiting for transfers between devices  9.71 us (32%)
  Pallas kernels  6.26 us (20%)
  between operations  0.77 us (3%)
    ppermute x5, waiting for transfers between devices, cross_swap(): lax.ppermute(array, 'fsdp', [(i, i ^ (odd if i % 2 else even)) for i in r...  7.91 us
    ppermute x5, starting transfers between devices, cross_swap(): lax.ppermute(array, 'fsdp', [(i, i ^ (odd if i % 2 else even)) for i in r...  7.57 us
    ppermute x4, starting transfers between devices, swap(): return lax.ppermute(array, 'fsdp', xor_pairs(lax.axis_size('fsdp'), mask))  3.52 us
    ppermute x1, starting transfers between devices, three_stage(): other = lax.ppermute(delta, 'replica', [(0, 1), (1, 0)])  2.56 us
    pallas_call x1, Pallas kernels, three_stage(): local_call(rows_kernel, 'token_rows', [((rows, features), bf16), ((2 * he...  2.46 us
    pallas_call x2, Pallas kernels, partial(): local_call(functools.partial(partial_kernel, tiles, own_half), 'partial_o...  1.65 us
    ppermute x4, waiting for transfers between devices, swap(): return lax.ppermute(array, 'fsdp', xor_pairs(lax.axis_size('fsdp'), mask))  0.96 us
    pallas_call x1, Pallas kernels, three_stage(): local_call(functools.partial(last_kernel, count), 'both_ends', [((1, chun...  0.91 us
  transfers between devices with their start and end apart: 10, of which 6 were waited for; matrix products, arithmetic and copies ran while one was open for 0% of the time, Pallas kernels for 7%

profile of v1, /device:TPU:0, one launch (start us, length us, event | category | flops | bytes accessed | tf_op | source)
XLA Modules:
  0.0 30.4 jit_solution(2509091835151116546)
XLA Ops:
  0.6 2.5 %token_rows.1 = (bf16[256,7168]{1,0:T(8,128)(2,1)S(1)}, bf16[256,256]{1,0:T(8,128)(2,1)S(1)}, bf16[2,4096]{1,0:T(2,128)(2,1)S(1)}) custom-call(bf16[256,7168]{1,0:T(8,128)(2,1)} %tokens.1, bf16[256,128]{1,0:T(8,128)(2,1)} %cotangent.1, s32[1,256]{1,0:T(1,128)} %bitcast.1, s32[8]{0:T(128)} %order.3, f32[1,8,4096]{2,1,0:T(8,128)} %local_params.3, ...), custom_call_target="tpu_custom_call" | custom-call | tf_op jit(solution)/shard_map/token_rows/pallas_call | solution.py:287
  3.1 0.8 %partial_far.1 = (bf16[112,16,128]{2,1,0:T(8,128)(2,1)S(1)}, f32[112,16,128]{2,1,0:T(8,128)S(1)}) custom-call(bf16[256,7168]{1,0:T(8,128)(2,1)S(1)} %get-tuple-element.31.held, bf16[256,256]{1,0:T(8,128)(2,1)S(1)} %get-tuple-element.32.left), custom_call_target="tpu_custom_call" | custom-call | bytes 4194304 | tf_op jit(solution)/shard_map/partial_far/pallas_call | solution.py:307
  3.9 0.0 copy-start.4
  3.9 0.5 %collective-permute-start = (bf16[112,16,128]{2,1,0:T(8,128)(2,1)S(1)}, bf16[112,16,128]{2,1,0:T(8,128)(2,1)S(1)}, u32[]{:S(2)}, u32[]{:S(2)}) collective-permute-start(bf16[112,16,128]{2,1,0:T(8,128)(2,1)S(1)} %get-tuple-element.35), channel_id=1, source_target_pairs={{0,1},{1,0},{2,3},{3,2},{4,5},{5,4},{6,7},{7,6},{8,9},{9,8},{10,11... | collective-permute-start | bytes 1376264 | tf_op jit(solution)/shard_map/ppermute | solution.py:46
  4.5 2.6 %collective-permute-start.1 = (bf16[2,4096]{1,0:T(2,128)(2,1)S(1)}, bf16[2,4096]{1,0:T(2,128)(2,1)S(1)}, u32[]{:S(2)}, u32[]{:S(2)}) collective-permute-start(bf16[2,4096]{1,0:T(2,128)(2,1)S(1)} %get-tuple-element.36.own), channel_id=1, source_target_pairs={{0,16},{16,0},{1,17},{17,1},{2,18},{18,2},{3,19},{19,3},{4,20},{20... | collective-permute-start | bytes 49160 | tf_op jit(solution)/shard_map/ppermute | solution.py:304
  7.0 0.8 %partial_own.1 = (bf16[112,16,128]{2,1,0:T(8,128)(2,1)S(1)}, f32[112,16,128]{2,1,0:T(8,128)S(1)}) custom-call(bf16[256,7168]{1,0:T(8,128)(2,1)S(1)} %get-tuple-element.31.held, bf16[256,256]{1,0:T(8,128)(2,1)S(1)} %get-tuple-element.32.left), custom_call_target="tpu_custom_call" | custom-call | bytes 4194304 | tf_op jit(solution)/shard_map/partial_own/pallas_call | solution.py:307
  7.9 0.0 copy-start
  7.9 0.0 copy-start.1
  7.9 0.0 copy-start.2
  7.9 0.0 copy-start.5
  7.9 0.0 copy-start.3
  7.9 0.8 %collective-permute-done.1.after.other = bf16[2,4096]{1,0:T(2,128)(2,1)S(1)} collective-permute-done((bf16[2,4096]{1,0:T(2,128)(2,1)S(1)}, bf16[2,4096]{1,0:T(2,128)(2,1)S(1)}, u32[]{:S(2)}, u32[]{:S(2)}) %collective-permute-start.1) | collective-permute-done | bytes 16416 | tf_op jit(solution)/shard_map/ppermute | solution.py:304
  8.8 0.1 first_far.1
  8.8 0.1 collective-permute-start.2
  8.9 2.1 %collective-permute-start.6 = (bf16[56,16,128]{2,1,0:T(8,128)(2,1)S(1)}, bf16[56,16,128]{2,1,0:T(8,128)(2,1)S(1)}, u32[]{:S(2)}, u32[]{:S(2)}) collective-permute-start(bf16[56,16,128]{2,1,0:T(8,128)(2,1)S(1)} %get-tuple-element.39.after), channel_id=1, source_target_pairs={{0,2},{1,5},{2,0},{3,7},{4,6},{5,1},{6,4},{7,3},{8,10},{9,13},{10,... | collective-permute-start | bytes 688136 | tf_op jit(solution)/shard_map/ppermute | solution.py:51
  11.0 0.1 gain_spread.1.after.spread
  11.2 0.2 squares.1.rest_0_
  11.3 0.3 collective-permute-start.3
  11.6 1.0 %collective-permute-done.3.rest_1_ = f32[8,128]{1,0:T(8,128)S(1)} collective-permute-done((f32[8,128]{1,0:T(8,128)S(1)}, f32[8,128]{1,0:T(8,128)S(1)}, u32[]{:S(2)}, u32[]{:S(2)}) %collective-permute-start.3) | collective-permute-done | bytes 4128 | tf_op jit(solution)/shard_map/ppermute | solution.py:46
  12.6 0.1 first_own.1
  12.7 1.4 %collective-permute-start.4 = (bf16[57,16,128]{2,1,0:T(8,128)(2,1)S(1)}, bf16[57,16,128]{2,1,0:T(8,128)(2,1)S(1)}, u32[]{:S(2)}, u32[]{:S(2)}) collective-permute-start(bf16[57,16,128]{2,1,0:T(8,128)(2,1)S(1)} %get-tuple-element.41), channel_id=1, source_target_pairs={{0,2},{1,5},{2,0},{3,7},{4,6},{5,1},{6,4},{7,3},{8,10},{9,13},{10,... | collective-permute-start | bytes 700424 | tf_op jit(solution)/shard_map/ppermute | solution.py:51
  14.1 0.9 %collective-permute-done.6.came = bf16[56,16,128]{2,1,0:T(8,128)(2,1)S(1)} collective-permute-done((bf16[56,16,128]{2,1,0:T(8,128)(2,1)S(1)}, bf16[56,16,128]{2,1,0:T(8,128)(2,1)S(1)}, u32[]{:S(2)}, u32[]{:S(2)}) %collective-permute-start.6) | collective-permute-done | bytes 229408 | tf_op jit(solution)/shard_map/ppermute | solution.py:51
  15.1 2.1 %collective-permute-start.7 = (bf16[28,16,128]{2,1,0:T(8,128)(2,1)S(1)}, bf16[28,16,128]{2,1,0:T(8,128)(2,1)S(1)}, u32[]{:S(2)}, u32[]{:S(2)}) collective-permute-start(bf16[28,16,128]{2,1,0:T(8,128)(2,1)S(1)} %get-tuple-element.49), channel_id=1, source_target_pairs={{0,4},{1,3},{2,6},{3,1},{4,0},{5,7},{6,2},{7,5},{8,12},{9,11},{10,... | collective-permute-start | bytes 344072 | tf_op jit(solution)/shard_map/ppermute | solution.py:51
  17.2 2.7 %collective-permute-done.4.came = bf16[57,16,128]{2,1,0:T(8,128)(2,1)S(1)} collective-permute-done((bf16[57,16,128]{2,1,0:T(8,128)(2,1)S(1)}, bf16[57,16,128]{2,1,0:T(8,128)(2,1)S(1)}, u32[]{:S(2)}, u32[]{:S(2)}) %collective-permute-start.4) | collective-permute-done | bytes 233504 | tf_op jit(solution)/shard_map/ppermute | solution.py:51
  19.9 0.1 second_own.1
  20.0 1.5 %collective-permute-start.5 = (bf16[29,16,128]{2,1,0:T(8,128)(2,1)S(1)}, bf16[29,16,128]{2,1,0:T(8,128)(2,1)S(1)}, u32[]{:S(2)}, u32[]{:S(2)}) collective-permute-start(bf16[29,16,128]{2,1,0:T(8,128)(2,1)S(1)} %get-tuple-element.44), channel_id=1, source_target_pairs={{0,4},{1,3},{2,6},{3,1},{4,0},{5,7},{6,2},{7,5},{8,12},{9,11},{10,... | collective-permute-start | bytes 356360 | tf_op jit(solution)/shard_map/ppermute | solution.py:51
  21.5 2.7 %collective-permute-start.8 = (bf16[29,16,128]{2,1,0:T(8,128)(2,1)S(1)}, bf16[29,16,128]{2,1,0:T(8,128)(2,1)S(1)}, u32[]{:S(2)}, u32[]{:S(2)}) collective-permute-start(bf16[29,16,128]{2,1,0:T(8,128)(2,1)S(1)} %third_far.1), channel_id=1, source_target_pairs={{0,8},{1,9},{2,10},{3,11},{4,12},{5,13},{6,14},{7,15},{8,0},{9,1},... | collective-permute-start | bytes 356360 | tf_op jit(solution)/shard_map/ppermute | solution.py:46
  24.1 0.4 %collective-permute-start.9 = (f32[8,128]{1,0:T(8,128)S(1)}, f32[8,128]{1,0:T(8,128)S(1)}, u32[]{:S(2)}, u32[]{:S(2)}) collective-permute-start(f32[8,128]{1,0:T(8,128)S(1)} %get-tuple-element.45.squares), channel_id=1, source_target_pairs={{0,12},{1,11},{2,14},{3,9},{4,8},{5,15},{6,10},{7,13},{8,4},{9,3},... | collective-permute-start | bytes 12296 | tf_op jit(solution)/shard_map/ppermute | solution.py:51
  24.5 1.8 %collective-permute-done.5.came = bf16[29,16,128]{2,1,0:T(8,128)(2,1)S(1)} collective-permute-done((bf16[29,16,128]{2,1,0:T(8,128)(2,1)S(1)}, bf16[29,16,128]{2,1,0:T(8,128)(2,1)S(1)}, u32[]{:S(2)}, u32[]{:S(2)}) %collective-permute-start.5) | collective-permute-done | bytes 118816 | tf_op jit(solution)/shard_map/ppermute | solution.py:51
  26.3 0.7 %prepare_ends.1 = (f32[28,16,128]{2,1,0:T(8,128)S(1)}, f32[8,128]{1,0:T(8,128)S(1)}, f32[1,8,4096]{2,1,0:T(8,128)S(1)}, f32[8,4096]{1,0:T(8,128)S(1)}, f32[8,409...) custom-call(f32[28,16,128]{2,1,0:T(8,128)S(1)} %get-tuple-element.43.keep, ...), custom_call_target="tpu_custom_call" | custom-call | tf_op jit(solution)/shard_map/prepare_ends/pallas_call | solution.py:359
  27.0 2.6 %collective-permute-done.9.squares_came = f32[8,128]{1,0:T(8,128)S(1)} collective-permute-done((f32[8,128]{1,0:T(8,128)S(1)}, f32[8,128]{1,0:T(8,128)S(1)}, u32[]{:S(2)}, u32[]{:S(2)}) %collective-permute-start.9) | collective-permute-done | bytes 4128 | tf_op jit(solution)/shard_map/ppermute | solution.py:51
  29.5 0.9 %both_ends.1 = (f32[1,448,128]{2,1,0:T(8,128)}, f32[1,448]{1,0:T(1,128)}, f32[1,8,4096]{2,1,0:T(8,128)}, f32[8,4096]{1,0:T(8,128)}, f32[8,4096]{1,0:T(8,128)}) custom-call(f32[28,16,128]{2,1,0:T(8,128)S(1)} %get-tuple-element.46.keep, bf16[29,16,128]{2,1,0:T(8,128)(2,1)S(1)} %collective-permute-done.8.came, f32[8,128]{1,0:T(8,128)S(1)} %get-tuple-element.50.squares, ...), custom_call_target="tpu_custom_call" | custom-call | tf_op jit(solution)/shard_map/both_ends/pallas_call | solution.py:368
  (12 shorter events, 0.1 us)
Async XLA Ops:
  3.9 7.1 %copy-start.4 = (f32[1,448]{1,0:T(1,128)S(1)}, f32[1,448]{1,0:T(1,128)}, u32[]{:S(2)}) copy-start(f32[1,448]{1,0:T(1,128)} %gain.1) | copy-start | bytes 5380
  3.9 4.8 %collective-permute-start = (bf16[112,16,128]{2,1,0:T(8,128)(2,1)S(1)}, bf16[112,16,128]{2,1,0:T(8,128)(2,1)S(1)}, u32[]{:S(2)}, u32[]{:S(2)}) collective-permute-start(bf16[112,16,128]{2,1,0:T(8,128)(2,1)S(1)} %get-tuple-element.35), channel_id=1, source_target_pairs={{0,1},{1,0},{2,3},{3,2},{4,5},{5,4},{6,7},{7,6},{8,9},{9,8},{10,11... | collective-permute-start | bytes 1376264 | tf_op jit(solution)/shard_map/ppermute | solution.py:46
  4.5 4.3 %collective-permute-start.1 = (bf16[2,4096]{1,0:T(2,128)(2,1)S(1)}, bf16[2,4096]{1,0:T(2,128)(2,1)S(1)}, u32[]{:S(2)}, u32[]{:S(2)}) collective-permute-start(bf16[2,4096]{1,0:T(2,128)(2,1)S(1)} %get-tuple-element.36.own), channel_id=1, source_target_pairs={{0,16},{16,0},{1,17},{17,1},{2,18},{18,2},{3,19},{19,3},{4,20},{20... | collective-permute-start | bytes 49160 | tf_op jit(solution)/shard_map/ppermute | solution.py:304
  7.9 18.4 %copy-start = (f32[1,8,4096]{2,1,0:T(8,128)S(1)}, f32[1,8,4096]{2,1,0:T(8,128)}, u32[]{:S(2)}) copy-start(f32[1,8,4096]{2,1,0:T(8,128)} %local_params.3) | copy-start | bytes 393220
  7.9 18.4 %copy-start.1 = (f32[8,4096]{1,0:T(8,128)S(1)}, f32[8,4096]{1,0:T(8,128)}, u32[]{:S(2)}) copy-start(f32[8,4096]{1,0:T(8,128)} %global_params.3) | copy-start | bytes 393220
  7.9 18.4 %copy-start.2 = (f32[8,4096]{1,0:T(8,128)S(1)}, f32[8,4096]{1,0:T(8,128)}, u32[]{:S(2)}) copy-start(f32[8,4096]{1,0:T(8,128)} %momentum.1) | copy-start | bytes 393220
  7.9 18.4 %copy-start.5 = (s32[8]{0:T(128)S(1)}, s32[8]{0:T(128)}, u32[]{:S(2)}) copy-start(s32[8]{0:T(128)} %order.3) | copy-start | bytes 100
  7.9 21.6 %copy-start.3 = (bf16[1,448,128]{2,1,0:T(8,128)(2,1)S(1)}, bf16[1,448,128]{2,1,0:T(8,128)(2,1)}, u32[]{:S(2)}) copy-start(bf16[1,448,128]{2,1,0:T(8,128)(2,1)} %weight.1) | copy-start | bytes 344068
  8.8 3.7 %collective-permute-start.2 = (bf16[112,16,128]{2,1,0:T(8,128)(2,1)S(1)}, bf16[112,16,128]{2,1,0:T(8,128)(2,1)S(1)}, u32[]{:S(2)}, u32[]{:S(2)}) collective-permute-start(bf16[112,16,128]{2,1,0:T(8,128)(2,1)S(1)} %get-tuple-element.38), channel_id=1, source_target_pairs={{0,1},{1,0},{2,3},{3,2},{4,5},{5,4},{6,7},{7,6},{8,9},{9,8},{10,11... | collective-permute-start | bytes 1376264 | tf_op jit(solution)/shard_map/ppermute | solution.py:46
  8.9 6.1 %collective-permute-start.6 = (bf16[56,16,128]{2,1,0:T(8,128)(2,1)S(1)}, bf16[56,16,128]{2,1,0:T(8,128)(2,1)S(1)}, u32[]{:S(2)}, u32[]{:S(2)}) collective-permute-start(bf16[56,16,128]{2,1,0:T(8,128)(2,1)S(1)} %get-tuple-element.39.after), channel_id=1, source_target_pairs={{0,2},{1,5},{2,0},{3,7},{4,6},{5,1},{6,4},{7,3},{8,10},{9,13},{10,... | collective-permute-start | bytes 688136 | tf_op jit(solution)/shard_map/ppermute | solution.py:51
  11.3 1.2 %collective-permute-start.3 = (f32[8,128]{1,0:T(8,128)S(1)}, f32[8,128]{1,0:T(8,128)S(1)}, u32[]{:S(2)}, u32[]{:S(2)}) collective-permute-start(f32[8,128]{1,0:T(8,128)S(1)} %squares.1.rest_0_), channel_id=1, source_target_pairs={{0,1},{1,0},{2,3},{3,2},{4,5},{5,4},{6,7},{7,6},{8,9},{9,8},{10,11... | collective-permute-start | bytes 12296 | tf_op jit(solution)/shard_map/ppermute | solution.py:46
  12.7 7.2 %collective-permute-start.4 = (bf16[57,16,128]{2,1,0:T(8,128)(2,1)S(1)}, bf16[57,16,128]{2,1,0:T(8,128)(2,1)S(1)}, u32[]{:S(2)}, u32[]{:S(2)}) collective-permute-start(bf16[57,16,128]{2,1,0:T(8,128)(2,1)S(1)} %get-tuple-element.41), channel_id=1, source_target_pairs={{0,2},{1,5},{2,0},{3,7},{4,6},{5,1},{6,4},{7,3},{8,10},{9,13},{10,... | collective-permute-start | bytes 700424 | tf_op jit(solution)/shard_map/ppermute | solution.py:51
  15.1 6.4 %collective-permute-start.7 = (bf16[28,16,128]{2,1,0:T(8,128)(2,1)S(1)}, bf16[28,16,128]{2,1,0:T(8,128)(2,1)S(1)}, u32[]{:S(2)}, u32[]{:S(2)}) collective-permute-start(bf16[28,16,128]{2,1,0:T(8,128)(2,1)S(1)} %get-tuple-element.49), channel_id=1, source_target_pairs={{0,4},{1,3},{2,6},{3,1},{4,0},{5,7},{6,2},{7,5},{8,12},{9,11},{10,... | collective-permute-start | bytes 344072 | tf_op jit(solution)/shard_map/ppermute | solution.py:51
  20.0 6.3 %collective-permute-start.5 = (bf16[29,16,128]{2,1,0:T(8,128)(2,1)S(1)}, bf16[29,16,128]{2,1,0:T(8,128)(2,1)S(1)}, u32[]{:S(2)}, u32[]{:S(2)}) collective-permute-start(bf16[29,16,128]{2,1,0:T(8,128)(2,1)S(1)} %get-tuple-element.44), channel_id=1, source_target_pairs={{0,4},{1,3},{2,6},{3,1},{4,0},{5,7},{6,2},{7,5},{8,12},{9,11},{10,... | collective-permute-start | bytes 356360 | tf_op jit(solution)/shard_map/ppermute | solution.py:51
  21.5 8.1 %collective-permute-start.8 = (bf16[29,16,128]{2,1,0:T(8,128)(2,1)S(1)}, bf16[29,16,128]{2,1,0:T(8,128)(2,1)S(1)}, u32[]{:S(2)}, u32[]{:S(2)}) collective-permute-start(bf16[29,16,128]{2,1,0:T(8,128)(2,1)S(1)} %third_far.1), channel_id=1, source_target_pairs={{0,8},{1,9},{2,10},{3,11},{4,12},{5,13},{6,14},{7,15},{8,0},{9,1},... | collective-permute-start | bytes 356360 | tf_op jit(solution)/shard_map/ppermute | solution.py:46
  24.1 5.4 %collective-permute-start.9 = (f32[8,128]{1,0:T(8,128)S(1)}, f32[8,128]{1,0:T(8,128)S(1)}, u32[]{:S(2)}, u32[]{:S(2)}) collective-permute-start(f32[8,128]{1,0:T(8,128)S(1)} %get-tuple-element.45.squares), channel_id=1, source_target_pairs={{0,12},{1,11},{2,14},{3,9},{4,8},{5,15},{6,10},{7,13},{8,4},{9,3},... | collective-permute-start | bytes 12296 | tf_op jit(solution)/shard_map/ppermute | solution.py:51

commit v2 on v1

--- a/solution.py
+++ b/solution.py
@@ -129,9 +129,7 @@
     mean = jnp.sum(squares[...].T, axis=0, keepdims=True) * (1.0 / width)
     scale = jnp.where(keep[...] == 1, lax.rsqrt(mean + EPSILON), 0.0)
     scaled = cot_t * scale
-    high = scaled.astype(jnp.bfloat16)
-    low = (scaled - high.astype(jnp.float32)).astype(jnp.bfloat16)
-    left[...] = jnp.concatenate([high, low], axis=0)
+    left[...] = scaled.astype(jnp.bfloat16)
 
 
 def place_bits():
@@ -154,7 +152,7 @@
         both = jnp.dot(
             left[...], held[:, pl.ds(start, 2 * chunk)], preferred_element_type=jnp.float32
         )
-        sums = (both[:heads] + both[heads:]).T.reshape(2, tiles, PACKED_ROWS, heads)
+        sums = both.T.reshape(2, tiles, PACKED_ROWS, heads)
         here = slice(k * tiles, (k + 1) * tiles)
         send[here] = jnp.where(first, sums[1], sums[0]).astype(jnp.bfloat16)
         keep[here] = jnp.where(first, sums[0], sums[1])
@@ -287,7 +285,7 @@
     held, left, delta = local_call(
         rows_kernel,
         "token_rows",
-        [((rows, features), bf16), ((2 * heads, rows), bf16), ((FRAG, width), bf16)],
+        [((rows, features), bf16), ((heads, rows), bf16), ((FRAG, width), bf16)],
         [HBM] * 6,
         24,
         [

time: 30.6 us -> 30.5 us (level)
  transfers between devices with their start and end apart: 10 -> 10, of which waited for: 6 -> 6; matrix products, arithmetic and copies ran while one was open for 0% -> 0% of each run, Pallas kernels for 7% -> 6%
where the time goes in v2:
time: 30.5 us; the launch traced here: 30.3 us
  starting transfers between devices  13.7 us (45%)
  waiting for transfers between devices  9.79 us (32%)
  Pallas kernels  6.07 us (20%)
  between operations  0.78 us (3%)
    ppermute x5, waiting for transfers between devices, cross_swap(): lax.ppermute(array, 'fsdp', [(i, i ^ (odd if i % 2 else even)) for i in r...  7.91 us
    ppermute x5, starting transfers between devices, cross_swap(): lax.ppermute(array, 'fsdp', [(i, i ^ (odd if i % 2 else even)) for i in r...  7.57 us
    ppermute x4, starting transfers between devices, swap(): return lax.ppermute(array, 'fsdp', xor_pairs(lax.axis_size('fsdp'), mask))  3.51 us
    ppermute x1, starting transfers between devices, three_stage(): other = lax.ppermute(delta, 'replica', [(0, 1), (1, 0)])  2.56 us
    pallas_call x1, Pallas kernels, three_stage(): local_call(rows_kernel, 'token_rows', [((rows, features), bf16), ((heads,...  2.44 us
    pallas_call x2, Pallas kernels, partial(): local_call(functools.partial(partial_kernel, tiles, own_half), 'partial_o...  1.48 us
    ppermute x4, waiting for transfers between devices, swap(): return lax.ppermute(array, 'fsdp', xor_pairs(lax.axis_size('fsdp'), mask))  0.96 us
    ppermute x1, waiting for transfers between devices, three_stage(): other = lax.ppermute(delta, 'replica', [(0, 1), (1, 0)])  0.92 us
  transfers between devices with their start and end apart: 10, of which 6 were waited for; matrix products, arithmetic and copies ran while one was open for 0% of the time, Pallas kernels for 6%

profile of v2, /device:TPU:0, one launch (start us, length us, event | category | flops | bytes accessed | tf_op | source)
XLA Modules:
  0.0 30.3 jit_solution(13953863658522619609)
XLA Ops:
  0.6 2.4 %token_rows.1 = (bf16[256,7168]{1,0:T(8,128)(2,1)S(1)}, bf16[128,256]{1,0:T(8,128)(2,1)S(1)}, bf16[2,4096]{1,0:T(2,128)(2,1)S(1)}) custom-call(bf16[256,7168]{1,0:T(8,128)(2,1)} %tokens.1, bf16[256,128]{1,0:T(8,128)(2,1)} %cotangent.1, s32[1,256]{1,0:T(1,128)} %bitcast.1, s32[8]{0:T(128)} %order.3, f32[1,8,4096]{2,1,0:T(8,128)} %local_params.3, ...), custom_call_target="tpu_custom_call" | custom-call | tf_op jit(solution)/shard_map/token_rows/pallas_call | solution.py:285
  3.1 0.8 %partial_far.1 = (bf16[112,16,128]{2,1,0:T(8,128)(2,1)S(1)}, f32[112,16,128]{2,1,0:T(8,128)S(1)}) custom-call(bf16[256,7168]{1,0:T(8,128)(2,1)S(1)} %get-tuple-element.31.held, bf16[128,256]{1,0:T(8,128)(2,1)S(1)} %get-tuple-element.32.left), custom_call_target="tpu_custom_call" | custom-call | bytes 4194304 | tf_op jit(solution)/shard_map/partial_far/pallas_call | solution.py:305
  3.8 0.0 copy-start.4
  3.8 0.5 %collective-permute-start = (bf16[112,16,128]{2,1,0:T(8,128)(2,1)S(1)}, bf16[112,16,128]{2,1,0:T(8,128)(2,1)S(1)}, u32[]{:S(2)}, u32[]{:S(2)}) collective-permute-start(bf16[112,16,128]{2,1,0:T(8,128)(2,1)S(1)} %get-tuple-element.35), channel_id=1, source_target_pairs={{0,1},{1,0},{2,3},{3,2},{4,5},{5,4},{6,7},{7,6},{8,9},{9,8},{10,11... | collective-permute-start | bytes 1376264 | tf_op jit(solution)/shard_map/ppermute | solution.py:46
  4.4 2.6 %collective-permute-start.1 = (bf16[2,4096]{1,0:T(2,128)(2,1)S(1)}, bf16[2,4096]{1,0:T(2,128)(2,1)S(1)}, u32[]{:S(2)}, u32[]{:S(2)}) collective-permute-start(bf16[2,4096]{1,0:T(2,128)(2,1)S(1)} %get-tuple-element.36.own), channel_id=1, source_target_pairs={{0,16},{16,0},{1,17},{17,1},{2,18},{18,2},{3,19},{19,3},{4,20},{20... | collective-permute-start | bytes 49160 | tf_op jit(solution)/shard_map/ppermute | solution.py:302
  6.9 0.7 %partial_own.1 = (bf16[112,16,128]{2,1,0:T(8,128)(2,1)S(1)}, f32[112,16,128]{2,1,0:T(8,128)S(1)}) custom-call(bf16[256,7168]{1,0:T(8,128)(2,1)S(1)} %get-tuple-element.31.held, bf16[128,256]{1,0:T(8,128)(2,1)S(1)} %get-tuple-element.32.left), custom_call_target="tpu_custom_call" | custom-call | bytes 4194304 | tf_op jit(solution)/shard_map/partial_own/pallas_call | solution.py:305
  7.7 0.0 copy-start
  7.7 0.0 copy-start.1
  7.7 0.0 copy-start.2
  7.7 0.0 copy-start.5
  7.7 0.0 copy-start.3
  7.7 0.9 %collective-permute-done.1.after.other = bf16[2,4096]{1,0:T(2,128)(2,1)S(1)} collective-permute-done((bf16[2,4096]{1,0:T(2,128)(2,1)S(1)}, bf16[2,4096]{1,0:T(2,128)(2,1)S(1)}, u32[]{:S(2)}, u32[]{:S(2)}) %collective-permute-start.1) | collective-permute-done | bytes 16416 | tf_op jit(solution)/shard_map/ppermute | solution.py:302
  8.7 0.1 first_far.1
  8.7 0.1 collective-permute-start.2
  8.8 2.1 %collective-permute-start.6 = (bf16[56,16,128]{2,1,0:T(8,128)(2,1)S(1)}, bf16[56,16,128]{2,1,0:T(8,128)(2,1)S(1)}, u32[]{:S(2)}, u32[]{:S(2)}) collective-permute-start(bf16[56,16,128]{2,1,0:T(8,128)(2,1)S(1)} %get-tuple-element.39.after), channel_id=1, source_target_pairs={{0,2},{1,5},{2,0},{3,7},{4,6},{5,1},{6,4},{7,3},{8,10},{9,13},{10,... | collective-permute-start | bytes 688136 | tf_op jit(solution)/shard_map/ppermute | solution.py:51
  10.9 0.1 gain_spread.1.after.spread
  11.1 0.2 squares.1.rest_0_
  11.2 0.3 collective-permute-start.3
  11.5 1.0 %collective-permute-done.3.rest_1_ = f32[8,128]{1,0:T(8,128)S(1)} collective-permute-done((f32[8,128]{1,0:T(8,128)S(1)}, f32[8,128]{1,0:T(8,128)S(1)}, u32[]{:S(2)}, u32[]{:S(2)}) %collective-permute-start.3) | collective-permute-done | bytes 4128 | tf_op jit(solution)/shard_map/ppermute | solution.py:46
  12.5 0.1 first_own.1
  12.6 1.4 %collective-permute-start.4 = (bf16[57,16,128]{2,1,0:T(8,128)(2,1)S(1)}, bf16[57,16,128]{2,1,0:T(8,128)(2,1)S(1)}, u32[]{:S(2)}, u32[]{:S(2)}) collective-permute-start(bf16[57,16,128]{2,1,0:T(8,128)(2,1)S(1)} %get-tuple-element.41), channel_id=1, source_target_pairs={{0,2},{1,5},{2,0},{3,7},{4,6},{5,1},{6,4},{7,3},{8,10},{9,13},{10,... | collective-permute-start | bytes 700424 | tf_op jit(solution)/shard_map/ppermute | solution.py:51
  14.0 0.9 %collective-permute-done.6.came = bf16[56,16,128]{2,1,0:T(8,128)(2,1)S(1)} collective-permute-done((bf16[56,16,128]{2,1,0:T(8,128)(2,1)S(1)}, bf16[56,16,128]{2,1,0:T(8,128)(2,1)S(1)}, u32[]{:S(2)}, u32[]{:S(2)}) %collective-permute-start.6) | collective-permute-done | bytes 229408 | tf_op jit(solution)/shard_map/ppermute | solution.py:51
  15.0 2.1 %collective-permute-start.7 = (bf16[28,16,128]{2,1,0:T(8,128)(2,1)S(1)}, bf16[28,16,128]{2,1,0:T(8,128)(2,1)S(1)}, u32[]{:S(2)}, u32[]{:S(2)}) collective-permute-start(bf16[28,16,128]{2,1,0:T(8,128)(2,1)S(1)} %get-tuple-element.49), channel_id=1, source_target_pairs={{0,4},{1,3},{2,6},{3,1},{4,0},{5,7},{6,2},{7,5},{8,12},{9,11},{10,... | collective-permute-start | bytes 344072 | tf_op jit(solution)/shard_map/ppermute | solution.py:51
  17.1 2.7 %collective-permute-done.4.came = bf16[57,16,128]{2,1,0:T(8,128)(2,1)S(1)} collective-permute-done((bf16[57,16,128]{2,1,0:T(8,128)(2,1)S(1)}, bf16[57,16,128]{2,1,0:T(8,128)(2,1)S(1)}, u32[]{:S(2)}, u32[]{:S(2)}) %collective-permute-start.4) | collective-permute-done | bytes 233504 | tf_op jit(solution)/shard_map/ppermute | solution.py:51
  19.8 0.1 second_own.1
  19.9 1.5 %collective-permute-start.5 = (bf16[29,16,128]{2,1,0:T(8,128)(2,1)S(1)}, bf16[29,16,128]{2,1,0:T(8,128)(2,1)S(1)}, u32[]{:S(2)}, u32[]{:S(2)}) collective-permute-start(bf16[29,16,128]{2,1,0:T(8,128)(2,1)S(1)} %get-tuple-element.44), channel_id=1, source_target_pairs={{0,4},{1,3},{2,6},{3,1},{4,0},{5,7},{6,2},{7,5},{8,12},{9,11},{10,... | collective-permute-start | bytes 356360 | tf_op jit(solution)/shard_map/ppermute | solution.py:51
  21.4 2.7 %collective-permute-start.8 = (bf16[29,16,128]{2,1,0:T(8,128)(2,1)S(1)}, bf16[29,16,128]{2,1,0:T(8,128)(2,1)S(1)}, u32[]{:S(2)}, u32[]{:S(2)}) collective-permute-start(bf16[29,16,128]{2,1,0:T(8,128)(2,1)S(1)} %third_far.1), channel_id=1, source_target_pairs={{0,8},{1,9},{2,10},{3,11},{4,12},{5,13},{6,14},{7,15},{8,0},{9,1},... | collective-permute-start | bytes 356360 | tf_op jit(solution)/shard_map/ppermute | solution.py:46
  24.0 0.4 %collective-permute-start.9 = (f32[8,128]{1,0:T(8,128)S(1)}, f32[8,128]{1,0:T(8,128)S(1)}, u32[]{:S(2)}, u32[]{:S(2)}) collective-permute-start(f32[8,128]{1,0:T(8,128)S(1)} %get-tuple-element.45.squares), channel_id=1, source_target_pairs={{0,12},{1,11},{2,14},{3,9},{4,8},{5,15},{6,10},{7,13},{8,4},{9,3},... | collective-permute-start | bytes 12296 | tf_op jit(solution)/shard_map/ppermute | solution.py:51
  24.4 1.8 %collective-permute-done.5.came = bf16[29,16,128]{2,1,0:T(8,128)(2,1)S(1)} collective-permute-done((bf16[29,16,128]{2,1,0:T(8,128)(2,1)S(1)}, bf16[29,16,128]{2,1,0:T(8,128)(2,1)S(1)}, u32[]{:S(2)}, u32[]{:S(2)}) %collective-permute-start.5) | collective-permute-done | bytes 118816 | tf_op jit(solution)/shard_map/ppermute | solution.py:51
  26.2 0.7 %prepare_ends.1 = (f32[28,16,128]{2,1,0:T(8,128)S(1)}, f32[8,128]{1,0:T(8,128)S(1)}, f32[1,8,4096]{2,1,0:T(8,128)S(1)}, f32[8,4096]{1,0:T(8,128)S(1)}, f32[8,409...) custom-call(f32[28,16,128]{2,1,0:T(8,128)S(1)} %get-tuple-element.43.keep, ...), custom_call_target="tpu_custom_call" | custom-call | tf_op jit(solution)/shard_map/prepare_ends/pallas_call | solution.py:357
  26.9 2.6 %collective-permute-done.9.squares_came = f32[8,128]{1,0:T(8,128)S(1)} collective-permute-done((f32[8,128]{1,0:T(8,128)S(1)}, f32[8,128]{1,0:T(8,128)S(1)}, u32[]{:S(2)}, u32[]{:S(2)}) %collective-permute-start.9) | collective-permute-done | bytes 4128 | tf_op jit(solution)/shard_map/ppermute | solution.py:51
  29.4 0.9 %both_ends.1 = (f32[1,448,128]{2,1,0:T(8,128)}, f32[1,448]{1,0:T(1,128)}, f32[1,8,4096]{2,1,0:T(8,128)}, f32[8,4096]{1,0:T(8,128)}, f32[8,4096]{1,0:T(8,128)}) custom-call(f32[28,16,128]{2,1,0:T(8,128)S(1)} %get-tuple-element.46.keep, bf16[29,16,128]{2,1,0:T(8,128)(2,1)S(1)} %collective-permute-done.8.came, f32[8,128]{1,0:T(8,128)S(1)} %get-tuple-element.50.squares, ...), custom_call_target="tpu_custom_call" | custom-call | tf_op jit(solution)/shard_map/both_ends/pallas_call | solution.py:366
  (12 shorter events, 0.1 us)
Async XLA Ops:
  3.8 7.1 %copy-start.4 = (f32[1,448]{1,0:T(1,128)S(1)}, f32[1,448]{1,0:T(1,128)}, u32[]{:S(2)}) copy-start(f32[1,448]{1,0:T(1,128)} %gain.1) | copy-start | bytes 5380
  3.8 4.8 %collective-permute-start = (bf16[112,16,128]{2,1,0:T(8,128)(2,1)S(1)}, bf16[112,16,128]{2,1,0:T(8,128)(2,1)S(1)}, u32[]{:S(2)}, u32[]{:S(2)}) collective-permute-start(bf16[112,16,128]{2,1,0:T(8,128)(2,1)S(1)} %get-tuple-element.35), channel_id=1, source_target_pairs={{0,1},{1,0},{2,3},{3,2},{4,5},{5,4},{6,7},{7,6},{8,9},{9,8},{10,11... | collective-permute-start | bytes 1376264 | tf_op jit(solution)/shard_map/ppermute | solution.py:46
  4.4 4.3 %collective-permute-start.1 = (bf16[2,4096]{1,0:T(2,128)(2,1)S(1)}, bf16[2,4096]{1,0:T(2,128)(2,1)S(1)}, u32[]{:S(2)}, u32[]{:S(2)}) collective-permute-start(bf16[2,4096]{1,0:T(2,128)(2,1)S(1)} %get-tuple-element.36.own), channel_id=1, source_target_pairs={{0,16},{16,0},{1,17},{17,1},{2,18},{18,2},{3,19},{19,3},{4,20},{20... | collective-permute-start | bytes 49160 | tf_op jit(solution)/shard_map/ppermute | solution.py:302
  7.7 18.5 %copy-start = (f32[1,8,4096]{2,1,0:T(8,128)S(1)}, f32[1,8,4096]{2,1,0:T(8,128)}, u32[]{:S(2)}) copy-start(f32[1,8,4096]{2,1,0:T(8,128)} %local_params.3) | copy-start | bytes 393220
  7.7 18.5 %copy-start.1 = (f32[8,4096]{1,0:T(8,128)S(1)}, f32[8,4096]{1,0:T(8,128)}, u32[]{:S(2)}) copy-start(f32[8,4096]{1,0:T(8,128)} %global_params.3) | copy-start | bytes 393220
  7.7 18.5 %copy-start.2 = (f32[8,4096]{1,0:T(8,128)S(1)}, f32[8,4096]{1,0:T(8,128)}, u32[]{:S(2)}) copy-start(f32[8,4096]{1,0:T(8,128)} %momentum.1) | copy-start | bytes 393220
  7.7 18.5 %copy-start.5 = (s32[8]{0:T(128)S(1)}, s32[8]{0:T(128)}, u32[]{:S(2)}) copy-start(s32[8]{0:T(128)} %order.3) | copy-start | bytes 100
  7.7 21.7 %copy-start.3 = (bf16[1,448,128]{2,1,0:T(8,128)(2,1)S(1)}, bf16[1,448,128]{2,1,0:T(8,128)(2,1)}, u32[]{:S(2)}) copy-start(bf16[1,448,128]{2,1,0:T(8,128)(2,1)} %weight.1) | copy-start | bytes 344068
  8.7 3.7 %collective-permute-start.2 = (bf16[112,16,128]{2,1,0:T(8,128)(2,1)S(1)}, bf16[112,16,128]{2,1,0:T(8,128)(2,1)S(1)}, u32[]{:S(2)}, u32[]{:S(2)}) collective-permute-start(bf16[112,16,128]{2,1,0:T(8,128)(2,1)S(1)} %get-tuple-element.38), channel_id=1, source_target_pairs={{0,1},{1,0},{2,3},{3,2},{4,5},{5,4},{6,7},{7,6},{8,9},{9,8},{10,11... | collective-permute-start | bytes 1376264 | tf_op jit(solution)/shard_map/ppermute | solution.py:46
  8.8 6.1 %collective-permute-start.6 = (bf16[56,16,128]{2,1,0:T(8,128)(2,1)S(1)}, bf16[56,16,128]{2,1,0:T(8,128)(2,1)S(1)}, u32[]{:S(2)}, u32[]{:S(2)}) collective-permute-start(bf16[56,16,128]{2,1,0:T(8,128)(2,1)S(1)} %get-tuple-element.39.after), channel_id=1, source_target_pairs={{0,2},{1,5},{2,0},{3,7},{4,6},{5,1},{6,4},{7,3},{8,10},{9,13},{10,... | collective-permute-start | bytes 688136 | tf_op jit(solution)/shard_map/ppermute | solution.py:51
  11.2 1.2 %collective-permute-start.3 = (f32[8,128]{1,0:T(8,128)S(1)}, f32[8,128]{1,0:T(8,128)S(1)}, u32[]{:S(2)}, u32[]{:S(2)}) collective-permute-start(f32[8,128]{1,0:T(8,128)S(1)} %squares.1.rest_0_), channel_id=1, source_target_pairs={{0,1},{1,0},{2,3},{3,2},{4,5},{5,4},{6,7},{7,6},{8,9},{9,8},{10,11... | collective-permute-start | bytes 12296 | tf_op jit(solution)/shard_map/ppermute | solution.py:46
  12.6 7.2 %collective-permute-start.4 = (bf16[57,16,128]{2,1,0:T(8,128)(2,1)S(1)}, bf16[57,16,128]{2,1,0:T(8,128)(2,1)S(1)}, u32[]{:S(2)}, u32[]{:S(2)}) collective-permute-start(bf16[57,16,128]{2,1,0:T(8,128)(2,1)S(1)} %get-tuple-element.41), channel_id=1, source_target_pairs={{0,2},{1,5},{2,0},{3,7},{4,6},{5,1},{6,4},{7,3},{8,10},{9,13},{10,... | collective-permute-start | bytes 700424 | tf_op jit(solution)/shard_map/ppermute | solution.py:51
  15.0 6.4 %collective-permute-start.7 = (bf16[28,16,128]{2,1,0:T(8,128)(2,1)S(1)}, bf16[28,16,128]{2,1,0:T(8,128)(2,1)S(1)}, u32[]{:S(2)}, u32[]{:S(2)}) collective-permute-start(bf16[28,16,128]{2,1,0:T(8,128)(2,1)S(1)} %get-tuple-element.49), channel_id=1, source_target_pairs={{0,4},{1,3},{2,6},{3,1},{4,0},{5,7},{6,2},{7,5},{8,12},{9,11},{10,... | collective-permute-start | bytes 344072 | tf_op jit(solution)/shard_map/ppermute | solution.py:51
  19.9 6.3 %collective-permute-start.5 = (bf16[29,16,128]{2,1,0:T(8,128)(2,1)S(1)}, bf16[29,16,128]{2,1,0:T(8,128)(2,1)S(1)}, u32[]{:S(2)}, u32[]{:S(2)}) collective-permute-start(bf16[29,16,128]{2,1,0:T(8,128)(2,1)S(1)} %get-tuple-element.44), channel_id=1, source_target_pairs={{0,4},{1,3},{2,6},{3,1},{4,0},{5,7},{6,2},{7,5},{8,12},{9,11},{10,... | collective-permute-start | bytes 356360 | tf_op jit(solution)/shard_map/ppermute | solution.py:51
  21.4 8.1 %collective-permute-start.8 = (bf16[29,16,128]{2,1,0:T(8,128)(2,1)S(1)}, bf16[29,16,128]{2,1,0:T(8,128)(2,1)S(1)}, u32[]{:S(2)}, u32[]{:S(2)}) collective-permute-start(bf16[29,16,128]{2,1,0:T(8,128)(2,1)S(1)} %third_far.1), channel_id=1, source_target_pairs={{0,8},{1,9},{2,10},{3,11},{4,12},{5,13},{6,14},{7,15},{8,0},{9,1},... | collective-permute-start | bytes 356360 | tf_op jit(solution)/shard_map/ppermute | solution.py:46
  24.0 5.4 %collective-permute-start.9 = (f32[8,128]{1,0:T(8,128)S(1)}, f32[8,128]{1,0:T(8,128)S(1)}, u32[]{:S(2)}, u32[]{:S(2)}) collective-permute-start(f32[8,128]{1,0:T(8,128)S(1)} %get-tuple-element.45.squares), channel_id=1, source_target_pairs={{0,12},{1,11},{2,14},{3,9},{4,8},{5,15},{6,10},{7,13},{8,4},{9,3},... | collective-permute-start | bytes 12296 | tf_op jit(solution)/shard_map/ppermute | solution.py:51
